TPU v7x, 512 devices: a whole 4x4x16 slice. The times are simulated.
512 devices in a mesh: tm: 32 (over z, core), row: 16 (over y, x).
Axes of the slice: x: 4, y: 4, z: 16, core: 2. Of those that a mesh axis runs over, the one named last changes fastest.
Arguments:
- covariance: float32 [32, 1024, 1024], P('tm', 'row'), as said below
- precision: float32 [32, 1024, 1024], P('tm', 'row'), as said below
- band_weight: float32 [32, 5, 1024], P('tm'), may hold values from -0.5 to 0.5
- band_offset: int32 [32, 5], P('tm'), may hold values from -64 to 64, as said below
- prior_mean: float32 [32, 1024], P('tm', 'row'), may hold values from -6 to 6
- innovation: float32 [32, 128], P('tm'), may hold values from -6 to 6
- seen_sites: int32 [32, 128], P('tm'), may hold values from 0 to 511, as said below
Outputs:
- smoother_gain: float32 [32, 1024, 1024], P('tm', 'row')
- smoother_shift: float32 [32, 1024], P('tm', 'row')
- smoother_spread: float32 [32, 1024, 1024], P('tm', 'row')
Inputs may be any that keep to these rules, and one draw needn't show every extreme that they name: `covariance`: each block's matrix is symmetric. `precision`: each block's matrix is symmetric. `band_offset`: the offsets of one block are distinct, and one of them has magnitude 64. `seen_sites`: the sites of one step are distinct.
All inputs are finite; a program needn't handle non-finite values.
Results may differ from a plain program's by a relative error of at most 0.0003.
Values sent between devices are 32-bit elements; how exact they have to be, the bound alone decides.
No kernel may reach another device: no remote copies, remote signals or barrier semaphores. Data moves between devices by JAX's collectives and lax.ppermute only.
A program may use at most 64 MiB of HBM per device.

v0:
```python
import jax
import jax.numpy as jnp
from jax import lax
from jax.sharding import PartitionSpec as P

NBAND = 5
REACH = 64
HIGHEST = lax.Precision.HIGHEST


def padded_2(cells, sides, width):
    for axis, dim in sides:
        count = lax.axis_size(axis)
        ends = count - 1
        head = lax.slice_in_dim(cells, 0, width, axis=dim)
        tail = lax.slice_in_dim(cells, cells.shape[dim] - width, cells.shape[dim], axis=dim)
        cells = jnp.concatenate(
            [
                lax.ppermute(tail, axis, [(i, (i + 1) % count) for i in range(ends)]),
                cells,
                lax.ppermute(head, axis, [((i + 1) % count, i) for i in range(ends)]),
            ],
            axis=dim,
        )
    return cells


def shifted(block, axis, distance):
    devices = range(lax.axis_size(axis))
    route = [(i - distance, i) for i in devices if i - distance in devices]
    return lax.ppermute(block, axis, route)


def product(left, right):
    return jnp.dot(left, right, precision=HIGHEST, preferred_element_type=jnp.float32)


def against(left, right):
    return lax.dot_general(
        left, right, (((1,), (1,)), ((), ())), precision=HIGHEST, preferred_element_type=jnp.float32
    )


def band_columns(matrix, weights, offsets):
    columns = matrix.shape[1]
    padded = jnp.pad(matrix, ((0, 0), (REACH, REACH)))
    summed = jnp.zeros(matrix.shape, jnp.float32)
    for band_index in range(NBAND):
        start_at = offsets[band_index] + REACH
        sliced = lax.dynamic_slice_in_dim(padded, start_at, columns, 1)
        summed = summed + weights[band_index][None, :] * sliced
    return summed


def body(covariance, precision, band_weight, band_offset, prior_mean, innovation, seen_sites):
    spread_rows = covariance[0]
    weights = band_weight[0]
    offsets = band_offset[0]
    local_rows = spread_rows.shape[0]
    columns = spread_rows.shape[1]
    first_local = lax.axis_index("row") * local_rows
    crossed = band_columns(spread_rows, weights, offsets)
    gain_rows = product(crossed, lax.all_gather(precision[0], "row", axis=0, tiled=True))
    matches = (seen_sites[0][:, None] == jnp.arange(columns, dtype=jnp.int32)[None, :]).astype(
        jnp.float32
    )
    pulled = product(innovation[0], matches)
    filtered = prior_mean[0] + product(spread_rows, pulled)
    rimmed = padded_2(filtered, (("row", 0),), REACH)
    local_weights = lax.dynamic_slice_in_dim(weights, first_local, local_rows, 1)
    forward = jnp.zeros((local_rows,), jnp.float32)
    for band_index in range(NBAND):
        start_at = offsets[band_index] + REACH
        forward = forward + local_weights[band_index] * lax.dynamic_slice_in_dim(
            rimmed, start_at, local_rows, 0
        )
    gain_full, forward_full = (
        lax.all_gather(gain_rows, "row", axis=0, tiled=True),
        lax.all_gather(forward, "row", axis=0, tiled=True),
    )
    spread_now = spread_rows - against(crossed, gain_full)
    shift_rows = filtered - product(gain_rows, forward_full)
    time_index = lax.axis_index("tm")
    time_count = lax.axis_size("tm")
    for stride in (1, 2):
        piece_gain, piece_shift, piece_spread = shifted(
            (gain_rows, shift_rows, spread_now), "tm", -stride
        )
        later_gain, later_shift, later_spread = (
            lax.all_gather(piece_gain, "row", axis=0, tiled=True),
            lax.all_gather(piece_shift, "row", axis=0, tiled=True),
            lax.all_gather(piece_spread, "row", axis=0, tiled=True),
        )
        merged_gain = product(gain_rows, later_gain)
        merged_shift = product(gain_rows, later_shift) + shift_rows
        merged_spread = against(product(gain_rows, later_spread), gain_full) + spread_now
        inside = time_index + stride < time_count
        if stride == 1:
            gain_full = jnp.where(inside, product(gain_full, later_gain), gain_full)
        gain_rows = jnp.where(inside, merged_gain, gain_rows)
        shift_rows = jnp.where(inside, merged_shift, shift_rows)
        spread_now = jnp.where(inside, merged_spread, spread_now)
    return (gain_rows[None], shift_rows[None], spread_now[None])


def solution(mesh):
    in_specs = (
        P("tm", "row", None),
        P("tm", "row", None),
        P("tm", None, None),
        P("tm", None),
        P("tm", "row"),
        P("tm", None),
        P("tm", None),
    )
    out_specs = (P("tm", "row", None), P("tm", "row"), P("tm", "row", None))
    return jax.shard_map(body, mesh=mesh, in_specs=in_specs, out_specs=out_specs, check_vma=False)
```

profile of v0, /device:TPU:96, one launch (start us, length us, event | category | flops | bytes accessed | tf_op | source)
XLA Modules:
  0.0 491.6 jit_solution(2502290297912747095)
XLA Ops:
  18.5 62.7 %all-gather.18.cloned.1.call-done = f32[1,1024,1024]{2,1,0:T(8,128)} async-done(((f32[1,64,1024]{2,1,0:T(8,128)}), f32[1,1024,1024]{2,1,0:T(8,128)}) %all-gather.18.cloned.1.call-update) | async-done | bytes 4194320 | tf_op jit(solution)/shard_map/all_gather | solution.py:63
  81.3 5.5 %fusion = f32[64,1024]{1,0:T(8,128)} fusion(f32[64,1024]{1,0:T(8,128)S(1)} %fusion.27, f32[1,1024,1024]{2,1,0:T(8,128)} %all-gather.18.cloned.1.call-done), kind=kOutput, calls=%fused_computation | convolution fusion | flops 805306368 | bytes 4718592 | tf_op jit(solution)/shard_map/dot_general | solution.py:35
  88.8 4.2 collective-permute-done
  93.8 59.8 %all-gather.12.cloned.1.call-done = f32[1024,1024]{1,0:T(8,128)} async-done(((f32[64,1024]{1,0:T(8,128)}), f32[1024,1024]{1,0:T(8,128)}) %all-gather.12.cloned.1.call-update) | async-done | bytes 4194320 | tf_op jit(solution)/shard_map/all_gather | solution.py:78
  153.6 6.3 %convolution_subtract_fusion = f32[64,1024]{1,0:T(8,128)S(1)} fusion(f32[64,1024]{1,0:T(8,128)S(1)} %fusion.27, f32[1024,1024]{1,0:T(8,128)} %all-gather.12.cloned.1.call-done, f32[1,64,1024]{2,1,0:T(8,128)S(1)} %copy-done.4), kind=kOutput, calls=%fused_computation.10 | convolution fusion | flops 805371904 | bytes 4980736 | tf_op jit(solution)/shard_map/dot_general | solution.py:39
  161.8 3.9 collective-permute-done.6
  166.5 57.4 %all-gather.8.cloned.1.call-done = f32[1024,1024]{1,0:T(8,128)} async-done(((f32[64,1024]{1,0:T(8,128)}), f32[1024,1024]{1,0:T(8,128)}) %all-gather.8.cloned.1.call-update) | async-done | bytes 4194320 | tf_op jit(solution)/shard_map/all_gather | solution.py:90
  223.9 4.8 convolution_select_fusion.1
  228.7 2.4 collective-permute-start.1
  231.1 8.8 %collective-permute-done.1 = f32[64,1024]{1,0:T(8,128)S(1)} collective-permute-done((f32[64,1024]{1,0:T(8,128)S(1)}, f32[64,1024]{1,0:T(8,128)S(1)}, u32[]{:S(2)}, u32[]{:S(2)}) %collective-permute-start.1) | collective-permute-done | bytes 262176 | tf_op jit(solution)/shard_map/ppermute | solution.py:31
  240.9 52.5 %all-gather.14.cloned.1.call-done = f32[1024,1024]{1,0:T(8,128)} async-done(((f32[64,1024]{1,0:T(8,128)}), f32[1024,1024]{1,0:T(8,128)}) %all-gather.14.cloned.1.call-update) | async-done | bytes 4194320 | tf_op jit(solution)/shard_map/all_gather | solution.py:92
  293.4 5.0 %fusion.52 = f32[64,1024]{1,0:T(8,128)S(1)} fusion(f32[64,1024]{1,0:T(8,128)S(1)} %copy-done.3, f32[1024,1024]{1,0:T(8,128)} %all-gather.14.cloned.1.call-done), kind=kOutput, calls=%fused_computation.67 | convolution fusion | flops 805306368 | bytes 4718592 | tf_op jit(solution)/shard_map/dot_general | solution.py:35
  298.4 4.1 fusion.6
  302.5 2.4 collective-permute-start.7
  304.9 8.8 %collective-permute-done.7 = f32[64,1024]{1,0:T(8,128)S(1)} collective-permute-done((f32[64,1024]{1,0:T(8,128)S(1)}, f32[64,1024]{1,0:T(8,128)S(1)}, u32[]{:S(2)}, u32[]{:S(2)}) %collective-permute-start.7) | collective-permute-done | bytes 262176 | tf_op jit(solution)/shard_map/ppermute | solution.py:31
  316.4 4.5 collective-permute-start.2
  327.1 37.3 %all-reduce.1 = f32[1024]{0:T(1024)S(1)} all-reduce(f32[1024]{0:T(1024)S(1)} %fusion.37), channel_id=1, replica_groups=mesh['tm'=32,'row'=16] {'row'}, use_global_device_ids=true, to_apply=%add.1 | all-reduce | flops 1024 | bytes 8192
  368.1 36.0 %all-reduce.2 = f32[1024]{0:T(1024)S(1)} all-reduce(f32[1024]{0:T(1024)S(1)} %dynamic-update-slice.1), channel_id=1, replica_groups=mesh['tm'=32,'row'=16] {'row'}, use_global_device_ids=true, to_apply=%add.2 | all-reduce | flops 1024 | bytes 8192
  406.4 4.7 collective-permute-done.5
  411.3 37.4 %all-reduce.3 = f32[1024]{0:T(1024)S(1)} all-reduce(f32[1024]{0:T(1024)S(1)} %dynamic-update-slice.2), channel_id=1, replica_groups=mesh['tm'=32,'row'=16] {'row'}, use_global_device_ids=true, to_apply=%add.3 | all-reduce | flops 1024 | bytes 8192
  449.5 17.5 %fusion.54 = f32[1024,1024]{1,0:T(8,128)} fusion(f32[1024,1024]{1,0:T(8,128)} %all-gather.12.cloned.1.call-done, f32[1024,1024]{1,0:T(8,128)} %all-gather.8.cloned.1.call-done), kind=kOutput, calls=%fused_computation.69 | convolution fusion | flops 12884901888 | bytes 12582912 | tf_op jit(solution)/shard_map/dot_general | solution.py:35
  467.0 5.5 %fusion.5 = f32[1,64,1024]{2,1,0:T(8,128)} fusion(f32[64,1024]{1,0:T(8,128)S(1)} %convolution_select_fusion.1, f32[1024,1024]{1,0:T(8,128)} %all-gather.10.cloned.1.call-done, pred[]{:T(512)S(6)} %lt.29), kind=kOutput, calls=%fused_computation.7 | convolution fusion | flops 805371904 | bytes 4718593 | tf_op jit(solution)/shard_map/dot_general | solution.py:35
  472.6 5.0 %fusion.53 = f32[64,1024]{1,0:T(8,128)S(1)} fusion(f32[64,1024]{1,0:T(8,128)S(1)} %convolution_select_fusion.1, f32[1024,1024]{1,0:T(8,128)} %all-gather.16.cloned.1.call-done), kind=kOutput, calls=%fused_computation.68 | convolution fusion | flops 805306368 | bytes 4718592 | tf_op jit(solution)/shard_map/dot_general | solution.py:35
  477.6 7.2 %fusion.13 = f32[1,64,1024]{2,1,0:T(8,128)} fusion(f32[64,1024]{1,0:T(8,128)S(1)} %fusion.6, f32[64,1024]{1,0:T(8,128)S(1)} %fusion.53, f32[1024,1024]{1,0:T(8,128)} %fusion.54, f32[1024,1024]{1,0:T(8,128)S(1)} %copy-done.2, pred[]{:T(512)S(6)} %lt.30, pred[]{:T(512)S(6)} %lt.29), kind=kOutput, calls=%fused_computation.13 | convolution fusion | flops 806486016 | bytes 9175042 | tf_op jit(solution)/shard_map/dot_general | solution.py:39
  (60 shorter events, 23.1 us)
Async XLA Ops:
  7.2 307.3 %copy-start = (f32[1,128]{1,0:T(1,128)S(1)}, f32[1,128]{1,0:T(1,128)}, u32[]{:S(2)}) copy-start(f32[1,128]{1,0:T(1,128)} %param.12) | copy-start | bytes 1540
  7.2 146.5 %copy-start.4 = (f32[1,64,1024]{2,1,0:T(8,128)S(1)}, f32[1,64,1024]{2,1,0:T(8,128)}, u32[]{:S(2)}) copy-start(f32[1,64,1024]{2,1,0:T(8,128)} %param.7) | copy-start | bytes 786436
  7.2 74.1 %all-gather.18.cloned.1.call-start = ((), (), s32[]{:S(2)}) async-start(), calls=%async_computation.5 | async-start | bytes 4456448 | tf_op jit(solution)/shard_map/all_gather | solution.py:63
  7.9 145.7 %all-gather.12.cloned.1.call-start = ((), (), s32[]{:S(2)}) async-start(), calls=%async_computation.2 | async-start | bytes 4456448 | tf_op jit(solution)/shard_map/all_gather | solution.py:78
  86.8 137.1 %copy-start.3 = (f32[64,1024]{1,0:T(8,128)S(1)}, f32[64,1024]{1,0:T(8,128)}, u32[]{:S(2)}) copy-start(f32[64,1024]{1,0:T(8,128)} %fusion) | copy-start | bytes 786436
  86.9 137.0 %all-gather.8.cloned.1.call-start = ((), (), s32[]{:S(2)}) async-start(), calls=%async_computation | async-start | bytes 4456448 | tf_op jit(solution)/shard_map/all_gather | solution.py:90
  86.9 6.1 %collective-permute-start = (f32[64,1024]{1,0:T(8,128)}, f32[64,1024]{1,0:T(8,128)S(1)}, u32[]{:S(2)}, u32[]{:S(2)}) collective-permute-start(f32[64,1024]{1,0:T(8,128)} %fusion), channel_id=1, source_target_pairs={{16,0},{32,16},{48,32},{64,48},{80,64},{96,80},{112,96},{128,112},... | collective-permute-start | bytes 786440 | tf_op jit(solution)/shard_map/ppermute | solution.py:31
  93.7 199.7 %all-gather.14.cloned.1.call-start = ((), (), s32[]{:S(2)}) async-start(), calls=%async_computation.3 | async-start | bytes 4456448 | tf_op jit(solution)/shard_map/all_gather | solution.py:92
  159.9 5.8 %collective-permute-start.6 = (f32[64,1024]{1,0:T(8,128)S(1)}, f32[64,1024]{1,0:T(8,128)S(1)}, u32[]{:S(2)}, u32[]{:S(2)}) collective-permute-start(f32[64,1024]{1,0:T(8,128)S(1)} %convolution_subtract_fusion), channel_id=1, source_target_pairs={{16,0},{32,16},{48,32},{64,48},{80,64},{96,80},{112,96},{128,112},... | collective-permute-start | bytes 786440 | tf_op jit(solution)/shard_map/ppermute | solution.py:31
  165.7 0.7 copy-start.8
  166.4 300.6 %all-gather.10.cloned.1.call-start = ((), (), s32[]{:S(2)}) async-start(), calls=%async_computation.1 | async-start | bytes 4456448 | tf_op jit(solution)/shard_map/all_gather | solution.py:90
  228.7 11.2 %collective-permute-start.1 = (f32[64,1024]{1,0:T(8,128)S(1)}, f32[64,1024]{1,0:T(8,128)S(1)}, u32[]{:S(2)}, u32[]{:S(2)}) collective-permute-start(f32[64,1024]{1,0:T(8,128)S(1)} %convolution_select_fusion.1), channel_id=1, source_target_pairs={{32,0},{48,16},{64,32},{80,48},{96,64},{112,80},{128,96},{144,112}... | collective-permute-start | bytes 786440 | tf_op jit(solution)/shard_map/ppermute | solution.py:31
  239.9 0.7 copy-start.5
  240.6 73.8 %copy-start.10 = (s32[1,128]{1,0:T(1,128)S(1)}, s32[1,128]{1,0:T(1,128)}, u32[]{:S(2)}) copy-start(s32[1,128]{1,0:T(1,128)} %param.13) | copy-start | bytes 1540
  240.6 74.1 %copy-start.9 = (f32[1,64]{1,0:T(1,128)S(1)}, f32[1,64]{1,0:T(1,128)}, u32[]{:S(2)}) copy-start(f32[1,64]{1,0:T(1,128)} %param.11) | copy-start | bytes 772
  240.6 231.9 %all-gather.16.cloned.1.call-start = ((), (), s32[]{:S(2)}) async-start(), calls=%async_computation.4 | async-start | bytes 4456448 | tf_op jit(solution)/shard_map/all_gather | solution.py:92
  293.4 5.0 %copy-start.1 = (f32[1024,1024]{1,0:T(8,128)S(1)}, f32[1024,1024]{1,0:T(8,128)}, u32[]{:S(2)}) copy-start(f32[1024,1024]{1,0:T(8,128)} %all-gather.12.cloned.1.call-done) | copy-start | bytes 12582916
  302.5 11.1 %collective-permute-start.7 = (f32[64,1024]{1,0:T(8,128)S(1)}, f32[64,1024]{1,0:T(8,128)S(1)}, u32[]{:S(2)}, u32[]{:S(2)}) collective-permute-start(f32[64,1024]{1,0:T(8,128)S(1)} %fusion.6), channel_id=1, source_target_pairs={{32,0},{48,16},{64,32},{80,48},{96,64},{112,80},{128,96},{144,112}... | collective-permute-start | bytes 786440 | tf_op jit(solution)/shard_map/ppermute | solution.py:31
  313.7 0.7 copy-start.6
  315.1 11.1 %collective-permute-start.3 = (f32[64]{0:T(128)S(1)}, f32[64]{0:T(128)S(1)}, u32[]{:S(2)}, u32[]{:S(2)}) collective-permute-start(f32[64]{0:T(128)S(1)} %fusion.22), channel_id=1, source_target_pairs={{1,0},{2,1},{3,2},{4,3},{5,4},{6,5},{7,6},{8,7},{9,8},{10,9},{11,1... | collective-permute-start | bytes 776 | tf_op jit(solution)/shard_map/ppermute | solution.py:21
  316.4 9.7 %collective-permute-start.2 = (f32[64]{0:T(128)S(1)}, f32[64]{0:T(128)S(1)}, u32[]{:S(2)}, u32[]{:S(2)}) collective-permute-start(f32[64]{0:T(128)S(1)} %fusion.22), channel_id=1, source_target_pairs={{0,1},{1,2},{2,3},{3,4},{4,5},{5,6},{6,7},{7,8},{8,9},{9,10},{10,1... | collective-permute-start | bytes 776 | tf_op jit(solution)/shard_map/ppermute | solution.py:19
  364.7 3.2 collective-permute-start.4
  404.4 6.7 %collective-permute-start.5 = (f32[64]{0:T(128)S(1)}, f32[64]{0:T(128)S(1)}, u32[]{:S(2)}, u32[]{:S(2)}) collective-permute-start(f32[64]{0:T(128)S(1)} %fusion.20), channel_id=1, source_target_pairs={{32,0},{48,16},{64,32},{80,48},{96,64},{112,80},{128,96},{144,112}... | collective-permute-start | bytes 776 | tf_op jit(solution)/shard_map/ppermute | solution.py:31
  472.6 5.0 %copy-start.2 = (f32[1024,1024]{1,0:T(8,128)S(1)}, f32[1024,1024]{1,0:T(8,128)}, u32[]{:S(2)}) copy-start(f32[1024,1024]{1,0:T(8,128)} %all-gather.12.cloned.1.call-done) | copy-start | bytes 12582916
  (1 other events, 0.7 us)
Sparse Core Ops, SparseCore 0:
  11.0 70.2 all-gather.17
  87.0 66.6 all-gather.11
  157.2 66.6 all-gather.7
  226.8 66.6 all-gather.13
  296.9 66.9 all-gather.9
  366.7 66.9 all-gather.15
where the time goes:
time: 492 us
  waiting for transfers between devices  265 us (54%)
  blocking collectives  111 us (23%)
  matrix products  62.9 us (13%)
  between operations  24.7 us (5%)
  starting transfers between devices  18.8 us (4%)
  local copies, waits for them, and re-layouts  6.74 us (1%)
    unnamed x3, blocking collectives  111 us
    all_gather x1, waiting for transfers between devices, body(): lax.all_gather(precision[0], 'row', axis=0, tiled=True)  62.7 us
    all_gather x1, waiting for transfers between devices, body(): lax.all_gather(gain_rows, 'row', axis=0, tiled=True)  59.8 us
    all_gather x2, waiting for transfers between devices, body(): lax.all_gather(piece_gain, 'row', axis=0, tiled=True)  57.4 us
    all_gather x2, waiting for transfers between devices, body(): lax.all_gather(piece_spread, 'row', axis=0, tiled=True)  52.6 us
    dot_general x11, matrix products, product(): jnp.dot(left, right, precision=HIGHEST, preferred_element_type=jnp.float32)  45.4 us
    ppermute x6, waiting for transfers between devices, shifted(): return lax.ppermute(block, axis, route)  31.6 us
    dot_general x3, matrix products, against(): lax.dot_general(left, right, (((1,), (1,)), ((), ())), precision=HIGHEST,...  17.6 us
  transfers between devices with their start and end apart: 14, of which 10 were waited for; matrix products, arithmetic and copies ran while one was open for 11% of the time, Pallas kernels for 0%

commit v1 on v0

--- a/solution.py
+++ b/solution.py
@@ -75,7 +75,9 @@
             rimmed, start_at, local_rows, 0
         )
     gain_full, forward_full = (
-        lax.all_gather(gain_rows, "row", axis=0, tiled=True),
+        jnp.concatenate(
+            lax.all_to_all(jnp.stack([gain_rows] * lax.axis_size("row")), "row", 0, 0), axis=0
+        ),
         lax.all_gather(forward, "row", axis=0, tiled=True),
     )
     spread_now = spread_rows - against(crossed, gain_full)

time: 492 us -> 457 us (0.929)
  waiting for transfers between devices: 265 us -> 168 us
  blocking collectives: 111 us -> 171 us
    all_to_all x0 -> x1, blocking collectives: none -> 60 us  [body(): lax.all_to_all(jnp.stack([gain_rows] * lax.axis_size('row')), 'row', 0, 0)]
    all_gather x1 -> x0, waiting for transfers between devices: 59.8 us -> none  [body(): lax.all_gather(gain_rows, 'row', axis=0, tiled=True)]
    all_gather x2, waiting for transfers between devices: 57.4 us -> 20.2 us  [body(): lax.all_gather(piece_gain, 'row', axis=0, tiled=True)]
  transfers between devices with their start and end apart: 14 -> 13, of which waited for: 10 -> 9; matrix products, arithmetic and copies ran while one was open for 11% -> 11% of each run, Pallas kernels for 0% -> 0%
where the time goes in v1:
time: 457 us; the launch traced here: 456 us
  blocking collectives  171 us (37%)
  waiting for transfers between devices  168 us (37%)
  matrix products  60.1 us (13%)
  between operations  24.4 us (5%)
  starting transfers between devices  20.7 us (5%)
  local copies, waits for them, and re-layouts  9.21 us (2%)
    unnamed x3, blocking collectives  111 us
    all_gather x1, waiting for transfers between devices, body(): lax.all_gather(precision[0], 'row', axis=0, tiled=True)  62.7 us
    all_to_all x1, blocking collectives, body(): lax.all_to_all(jnp.stack([gain_rows] * lax.axis_size('row')), 'row', 0, 0)  60 us
    all_gather x2, waiting for transfers between devices, body(): lax.all_gather(piece_spread, 'row', axis=0, tiled=True)  53.3 us
    dot_general x11, matrix products, product(): jnp.dot(left, right, precision=HIGHEST, preferred_element_type=jnp.float32)  44.7 us
    ppermute x6, waiting for transfers between devices, shifted(): return lax.ppermute(block, axis, route)  31.2 us
    all_gather x2, waiting for transfers between devices, body(): lax.all_gather(piece_gain, 'row', axis=0, tiled=True)  20.2 us
    dot_general x3, matrix products, against(): lax.dot_general(left, right, (((1,), (1,)), ((), ())), precision=HIGHEST,...  15.4 us
  transfers between devices with their start and end apart: 13, of which 9 were waited for; matrix products, arithmetic and copies ran while one was open for 11% of the time, Pallas kernels for 0%

profile of v1, /device:TPU:96, one launch (start us, length us, event | category | flops | bytes accessed | tf_op | source)
XLA Modules:
  0.0 456.1 jit_solution(7597621127712083354)
XLA Ops:
  18.6 62.7 %all-gather.15.cloned.1.call-done = f32[1,1024,1024]{2,1,0:T(8,128)} async-done(((f32[1,64,1024]{2,1,0:T(8,128)}), f32[1,1024,1024]{2,1,0:T(8,128)}) %all-gather.15.cloned.1.call-update) | async-done | bytes 4194320 | tf_op jit(solution)/shard_map/all_gather | solution.py:63
  81.3 4.8 %fusion = f32[64,1024]{1,0:T(8,128)S(1)} fusion(f32[64,1024]{1,0:T(8,128)S(1)} %fusion.27, f32[1,1024,1024]{2,1,0:T(8,128)} %all-gather.15.cloned.1.call-done), kind=kOutput, calls=%fused_computation | convolution fusion | flops 805306368 | bytes 4718592 | tf_op jit(solution)/shard_map/dot_general | solution.py:35
  88.1 3.9 collective-permute-done
  93.2 60.0 %all_to_all.5 = f32[16,64,1024]{2,1,0:T(8,128)S(1)} all-to-all(f32[16,64,1024]{2,1,0:T(8,128)S(1)} %stack.2), channel_id=1, replica_groups=mesh['tm'=32,'row'=16] {'row'}, dimensions={0} | all-to-all | bytes 8388608 | tf_op jit(solution)/shard_map/all_to_all | solution.py:79
  155.2 4.1 convolution_subtract_fusion
  159.3 3.8 collective-permute-start.6
  163.1 3.9 collective-permute-done.6
  167.7 20.2 %all-gather.7.cloned.1.call-done = f32[1024,1024]{1,0:T(8,128)} async-done(((f32[64,1024]{1,0:T(8,128)}), f32[1024,1024]{1,0:T(8,128)}) %all-gather.7.cloned.1.call-update) | async-done | bytes 4194320 | tf_op jit(solution)/shard_map/all_gather | solution.py:92
  188.0 4.8 %convolution_select_fusion.1 = f32[64,1024]{1,0:T(8,128)S(1)} fusion(f32[64,1024]{1,0:T(8,128)S(1)} %fusion, f32[1024,1024]{1,0:T(8,128)} %all-gather.7.cloned.1.call-done, pred[]{:T(512)S(6)} %lt.30), kind=kOutput, calls=%fused_computation.6 | convolution fusion | flops 805371904 | bytes 4718593 | tf_op jit(solution)/shard_map/dot_general | solution.py:35
  192.8 2.4 collective-permute-start.1
  195.2 8.8 %collective-permute-done.1 = f32[64,1024]{1,0:T(8,128)S(1)} collective-permute-done((f32[64,1024]{1,0:T(8,128)S(1)}, f32[64,1024]{1,0:T(8,128)S(1)}, u32[]{:S(2)}, u32[]{:S(2)}) %collective-permute-start.1) | collective-permute-done | bytes 262176 | tf_op jit(solution)/shard_map/ppermute | solution.py:31
  205.0 53.3 %all-gather.11.cloned.1.call-done = f32[1024,1024]{1,0:T(8,128)} async-done(((f32[64,1024]{1,0:T(8,128)}), f32[1024,1024]{1,0:T(8,128)}) %all-gather.11.cloned.1.call-update) | async-done | bytes 4194320 | tf_op jit(solution)/shard_map/all_gather | solution.py:94
  258.2 5.0 %fusion.52 = f32[64,1024]{1,0:T(8,128)S(1)} fusion(f32[64,1024]{1,0:T(8,128)S(1)} %fusion, f32[1024,1024]{1,0:T(8,128)} %all-gather.11.cloned.1.call-done), kind=kOutput, calls=%fused_computation.67 | convolution fusion | flops 805306368 | bytes 4718592 | tf_op jit(solution)/shard_map/dot_general | solution.py:35
  263.2 4.1 fusion.6
  269.7 8.8 %collective-permute-done.7 = f32[64,1024]{1,0:T(8,128)S(1)} collective-permute-done((f32[64,1024]{1,0:T(8,128)S(1)}, f32[64,1024]{1,0:T(8,128)S(1)}, u32[]{:S(2)}, u32[]{:S(2)}) %collective-permute-start.7) | collective-permute-done | bytes 262176 | tf_op jit(solution)/shard_map/ppermute | solution.py:31
  281.2 4.5 collective-permute-start.2
  291.9 37.3 %all-reduce.1 = f32[1024]{0:T(1024)S(1)} all-reduce(f32[1024]{0:T(1024)S(1)} %fusion.37), channel_id=1, replica_groups=mesh['tm'=32,'row'=16] {'row'}, use_global_device_ids=true, to_apply=%add.1 | all-reduce | flops 1024 | bytes 8192
  332.9 36.0 %all-reduce.2 = f32[1024]{0:T(1024)S(1)} all-reduce(f32[1024]{0:T(1024)S(1)} %dynamic-update-slice.1), channel_id=1, replica_groups=mesh['tm'=32,'row'=16] {'row'}, use_global_device_ids=true, to_apply=%add.2 | all-reduce | flops 1024 | bytes 8192
  371.2 4.7 %collective-permute-done.5 = f32[64]{0:T(128)S(1)} collective-permute-done((f32[64]{0:T(128)S(1)}, f32[64]{0:T(128)S(1)}, u32[]{:S(2)}, u32[]{:S(2)}) %collective-permute-start.5) | collective-permute-done | bytes 288 | tf_op jit(solution)/shard_map/ppermute | solution.py:31
  376.1 37.4 %all-reduce.3 = f32[1024]{0:T(1024)S(1)} all-reduce(f32[1024]{0:T(1024)S(1)} %dynamic-update-slice.2), channel_id=1, replica_groups=mesh['tm'=32,'row'=16] {'row'}, use_global_device_ids=true, to_apply=%add.3 | all-reduce | flops 1024 | bytes 8192
  414.3 17.6 %fusion.54 = f32[1024,1024]{1,0:T(8,128)} fusion(f32[1024,1024]{1,0:T(8,128)} %bitcast.132, f32[1024,1024]{1,0:T(8,128)} %all-gather.7.cloned.1.call-done), kind=kOutput, calls=%fused_computation.69 | convolution fusion | flops 12884901888 | bytes 12582912 | tf_op jit(solution)/shard_map/dot_general | solution.py:35
  431.9 5.5 %fusion.5 = f32[1,64,1024]{2,1,0:T(8,128)} fusion(f32[64,1024]{1,0:T(8,128)S(1)} %convolution_select_fusion.1, f32[1024,1024]{1,0:T(8,128)} %all-gather.9.cloned.1.call-done, pred[]{:T(512)S(6)} %lt.29), kind=kOutput, calls=%fused_computation.7 | convolution fusion | flops 805371904 | bytes 4718593 | tf_op jit(solution)/shard_map/dot_general | solution.py:35
  437.4 5.0 %fusion.53 = f32[64,1024]{1,0:T(8,128)S(1)} fusion(f32[64,1024]{1,0:T(8,128)S(1)} %convolution_select_fusion.1, f32[1024,1024]{1,0:T(8,128)} %all-gather.13.cloned.1.call-done), kind=kOutput, calls=%fused_computation.68 | convolution fusion | flops 805306368 | bytes 4718592 | tf_op jit(solution)/shard_map/dot_general | solution.py:35
  442.4 7.2 %fusion.13 = f32[1,64,1024]{2,1,0:T(8,128)} fusion(f32[64,1024]{1,0:T(8,128)S(1)} %fusion.6, f32[64,1024]{1,0:T(8,128)S(1)} %fusion.53, f32[1024,1024]{1,0:T(8,128)} %fusion.54, f32[1024,1024]{1,0:T(8,128)S(1)} %bitcast.134, pred[]{:T(512)S(6)} %lt.30, pred[]{:T(512)S(6)} %lt.29), kind=kOutput, calls=%fused_computation.13 | convolution fusion | flops 806486016 | bytes 9175042 | tf_op jit(solution)/shard_map/dot_general | solution.py:39
  (59 shorter events, 26.0 us)
Async XLA Ops:
  7.2 272.1 %copy-start = (f32[1,128]{1,0:T(1,128)S(1)}, f32[1,128]{1,0:T(1,128)}, u32[]{:S(2)}) copy-start(f32[1,128]{1,0:T(1,128)} %param.12) | copy-start | bytes 1540
  7.2 74.1 %all-gather.15.cloned.1.call-start = ((), (), s32[]{:S(2)}) async-start(), calls=%async_computation.5 | async-start | bytes 4456448 | tf_op jit(solution)/shard_map/all_gather | solution.py:63
  7.9 180.1 %all-gather.7.cloned.1.call-start = ((), (), s32[]{:S(2)}) async-start(), calls=%async_computation.1 | async-start | bytes 4456448 | tf_op jit(solution)/shard_map/all_gather | solution.py:92
  86.1 5.8 %collective-permute-start = (f32[64,1024]{1,0:T(8,128)S(1)}, f32[64,1024]{1,0:T(8,128)S(1)}, u32[]{:S(2)}, u32[]{:S(2)}) collective-permute-start(f32[64,1024]{1,0:T(8,128)S(1)} %fusion), channel_id=1, source_target_pairs={{16,0},{32,16},{48,32},{64,48},{80,64},{96,80},{112,96},{128,112},... | collective-permute-start | bytes 786440 | tf_op jit(solution)/shard_map/ppermute | solution.py:31
  91.9 0.7 copy-start.7
  92.6 165.6 %all-gather.11.cloned.1.call-start = ((), (), s32[]{:S(2)}) async-start(), calls=%async_computation.3 | async-start | bytes 4456448 | tf_op jit(solution)/shard_map/all_gather | solution.py:94
  93.2 62.0 %copy-start.4 = (f32[1,64,1024]{2,1,0:T(8,128)S(1)}, f32[1,64,1024]{2,1,0:T(8,128)}, u32[]{:S(2)}) copy-start(f32[1,64,1024]{2,1,0:T(8,128)} %param.7) | copy-start | bytes 786436
  153.2 2.0 copy-start.1
  159.3 7.7 %collective-permute-start.6 = (f32[64,1024]{1,0:T(8,128)S(1)}, f32[64,1024]{1,0:T(8,128)S(1)}, u32[]{:S(2)}, u32[]{:S(2)}) collective-permute-start(f32[64,1024]{1,0:T(8,128)S(1)} %convolution_subtract_fusion), channel_id=1, source_target_pairs={{16,0},{32,16},{48,32},{64,48},{80,64},{96,80},{112,96},{128,112},... | collective-permute-start | bytes 786440 | tf_op jit(solution)/shard_map/ppermute | solution.py:31
  167.0 0.7 copy-start.8
  167.7 264.2 %all-gather.9.cloned.1.call-start = ((), (), s32[]{:S(2)}) async-start(), calls=%async_computation.2 | async-start | bytes 4456448 | tf_op jit(solution)/shard_map/all_gather | solution.py:92
  192.8 11.2 %collective-permute-start.1 = (f32[64,1024]{1,0:T(8,128)S(1)}, f32[64,1024]{1,0:T(8,128)S(1)}, u32[]{:S(2)}, u32[]{:S(2)}) collective-permute-start(f32[64,1024]{1,0:T(8,128)S(1)} %convolution_select_fusion.1), channel_id=1, source_target_pairs={{32,0},{48,16},{64,32},{80,48},{96,64},{112,80},{128,96},{144,112}... | collective-permute-start | bytes 786440 | tf_op jit(solution)/shard_map/ppermute | solution.py:31
  204.0 0.7 copy-start.5
  204.7 74.5 %copy-start.10 = (s32[1,128]{1,0:T(1,128)S(1)}, s32[1,128]{1,0:T(1,128)}, u32[]{:S(2)}) copy-start(s32[1,128]{1,0:T(1,128)} %param.13) | copy-start | bytes 1540
  204.7 74.9 %copy-start.9 = (f32[1,64]{1,0:T(1,128)S(1)}, f32[1,64]{1,0:T(1,128)}, u32[]{:S(2)}) copy-start(f32[1,64]{1,0:T(1,128)} %param.11) | copy-start | bytes 772
  204.7 232.7 %all-gather.13.cloned.1.call-start = ((), (), s32[]{:S(2)}) async-start(), calls=%async_computation.4 | async-start | bytes 4456448 | tf_op jit(solution)/shard_map/all_gather | solution.py:94
  258.2 5.0 %copy-start.2 = (f32[16,64,1024]{2,1,0:T(8,128)S(1)}, f32[16,64,1024]{2,1,0:T(8,128)}, u32[]{:S(2)}) copy-start(f32[16,64,1024]{2,1,0:T(8,128)} %copy-done.1) | copy-start | bytes 12582916
  267.4 11.1 %collective-permute-start.7 = (f32[64,1024]{1,0:T(8,128)S(1)}, f32[64,1024]{1,0:T(8,128)S(1)}, u32[]{:S(2)}, u32[]{:S(2)}) collective-permute-start(f32[64,1024]{1,0:T(8,128)S(1)} %fusion.6), channel_id=1, source_target_pairs={{32,0},{48,16},{64,32},{80,48},{96,64},{112,80},{128,96},{144,112}... | collective-permute-start | bytes 786440 | tf_op jit(solution)/shard_map/ppermute | solution.py:31
  278.5 0.7 copy-start.6
  279.9 11.1 %collective-permute-start.3 = (f32[64]{0:T(128)S(1)}, f32[64]{0:T(128)S(1)}, u32[]{:S(2)}, u32[]{:S(2)}) collective-permute-start(f32[64]{0:T(128)S(1)} %fusion.22), channel_id=1, source_target_pairs={{1,0},{2,1},{3,2},{4,3},{5,4},{6,5},{7,6},{8,7},{9,8},{10,9},{11,1... | collective-permute-start | bytes 776 | tf_op jit(solution)/shard_map/ppermute | solution.py:21
  281.2 9.7 %collective-permute-start.2 = (f32[64]{0:T(128)S(1)}, f32[64]{0:T(128)S(1)}, u32[]{:S(2)}, u32[]{:S(2)}) collective-permute-start(f32[64]{0:T(128)S(1)} %fusion.22), channel_id=1, source_target_pairs={{0,1},{1,2},{2,3},{3,4},{4,5},{5,6},{6,7},{7,8},{8,9},{9,10},{10,1... | collective-permute-start | bytes 776 | tf_op jit(solution)/shard_map/ppermute | solution.py:19
  329.5 3.2 collective-permute-start.4
  369.2 6.7 %collective-permute-start.5 = (f32[64]{0:T(128)S(1)}, f32[64]{0:T(128)S(1)}, u32[]{:S(2)}, u32[]{:S(2)}) collective-permute-start(f32[64]{0:T(128)S(1)} %fusion.20), channel_id=1, source_target_pairs={{32,0},{48,16},{64,32},{80,48},{96,64},{112,80},{128,96},{144,112}... | collective-permute-start | bytes 776 | tf_op jit(solution)/shard_map/ppermute | solution.py:31
  437.4 5.0 %copy-start.3 = (f32[16,64,1024]{2,1,0:T(8,128)S(1)}, f32[16,64,1024]{2,1,0:T(8,128)}, u32[]{:S(2)}) copy-start(f32[16,64,1024]{2,1,0:T(8,128)} %copy-done.1) | copy-start | bytes 12582916
Sparse Core Ops, SparseCore 0:
  11.0 70.2 all-gather.14
  92.8 95.1 all-gather.6
  191.6 66.6 all-gather.10
  261.7 66.9 all-gather.8
  331.6 66.9 all-gather.12
